TPU v7x, 512 devices: a whole 4x4x16 slice. The times are simulated.
512 devices in a mesh: chan: 128 (over y, z, x_hi), pair: 4 (over x_lo, core).
Axes of the slice: x: 4 (x_hi: 2, x_lo: 2; x = x_hi * 2 + x_lo), y: 4, z: 16, core: 2. Of those that a mesh axis runs over, the one named last changes fastest.
Arguments:
- voltages: bfloat16 [4, 256, 2, 34560], P('pair', 'chan'), may hold values from -6 to 6
- fir_taps: float32 [8, 256], replicated, may hold values from -2 to 2
Outputs:
- visibilities: float32 [128, 2, 1024, 1024], P('chan', None, 'pair')
All inputs are finite; a program needn't handle non-finite values.
Results may differ from a plain program's by a relative error of at most 0.0036.
Values may be sent and summed in bfloat16 or wider, within the bound.
A program may use at most 64 MiB of HBM per device.

v0:
```python
import math
import jax
import jax.numpy as jnp
from jax import lax
from jax.sharding import PartitionSpec as P


def dft_rows(channels):
    frame = 2 * channels
    row_index = jnp.arange(2 * channels, dtype=jnp.int32)
    col_index = jnp.arange(frame, dtype=jnp.int32)
    freq_index = row_index // 2
    phases = freq_index[:, None] * col_index[None, :] % frame
    angles = phases.astype(jnp.float32) * (2.0 * math.pi / frame)
    chosen = jnp.where((row_index % 2 == 0)[:, None], jnp.cos(angles), -jnp.sin(angles))
    return chosen * (1.0 / math.sqrt(frame))


def channelize(sample_rows, fir_taps, transform, spectra_len):
    tap_count, frame = fir_taps.shape
    channels = frame // 2
    framed = sample_rows.astype(jnp.float32).reshape(
        sample_rows.shape[0], spectra_len + tap_count - 1, frame
    )
    filtered = jnp.zeros((sample_rows.shape[0], spectra_len, frame), jnp.float32)
    for tap in range(tap_count):
        filtered = filtered + fir_taps[tap][None, None, :] * framed[:, tap : tap + spectra_len, :]
    spectra = jnp.einsum("wn,asn->aws", transform, filtered, precision=lax.Precision.HIGHEST)
    return spectra.reshape(sample_rows.shape[0], channels, 2 * spectra_len).astype(jnp.bfloat16)


def correlate(own_rows, columns, spectra_len):
    blocks = columns.shape[2] // (2 * spectra_len)
    shaped = columns.reshape(columns.shape[0], columns.shape[1], blocks, 2, spectra_len)
    rotated = jnp.stack([-shaped[:, :, :, 1, :], shaped[:, :, :, 0, :]], axis=3).reshape(
        columns.shape
    )
    stacked = jnp.concatenate([columns, rotated], axis=0)
    stacked = jnp.transpose(stacked, (1, 0, 2))
    own_first = jnp.transpose(own_rows, (1, 0, 2))
    product = jnp.einsum("cik,cjk->cij", own_first, stacked, preferred_element_type=jnp.float32)
    count = columns.shape[0]
    product = product.reshape(product.shape[0], product.shape[1], 2, count)
    return jnp.transpose(product, (0, 2, 1, 3))


def shards(voltages, fir_taps):
    samples = voltages[0]
    batch_count = samples.shape[1]
    tap_count, frame = fir_taps.shape
    spectra_len = samples.shape[2] // frame - tap_count + 1
    transform = dft_rows(frame // 2)
    pieces = [
        channelize(samples[:, batch], fir_taps, transform, spectra_len)
        for batch in range(batch_count)
    ]
    spectra = jnp.concatenate(pieces, axis=2)[None]
    gathered = lax.all_gather(spectra, "pair", axis=0, tiled=True)
    turned = lax.all_to_all(gathered, "chan", split_axis=2, concat_axis=1, tiled=True)
    everyone = turned.reshape(turned.shape[0] * turned.shape[1], turned.shape[2], turned.shape[3])
    own_rows = lax.dynamic_index_in_dim(turned, lax.axis_index("pair"), 0, keepdims=False)
    summed = correlate(own_rows, everyone, spectra_len)
    return summed * (1.0 / math.sqrt(batch_count * spectra_len))


def solution(mesh):
    in_specs = (P("pair", "chan", None, None), P())
    out_specs = P("chan", None, "pair", None)
    return jax.shard_map(shards, mesh=mesh, in_specs=in_specs, out_specs=out_specs, check_vma=False)
```

profile of v0, /device:TPU:8, one launch (start us, length us, event | category | flops | bytes accessed | tf_op | source)
XLA Modules:
  0.0 145.8 jit_solution(16215200199921057058)
XLA Ops:
  6.5 0.0 all-gather.3.cloned.1.call-start
  6.5 1.0 fusion.70
  7.5 2.8 %fusion.3 = (f32[2,34560]{1,0:T(2,128)S(1)}, f32[2,34560]{1,0:T(2,128)S(1)}) fusion(bf16[2,2,34560]{2,1,0:T(2,128)(2,1)} %bitcast.42), kind=kLoop, calls=%fused_computation.14 | loop fusion | flops 138240 | bytes 829440 | tf_op jit(solution)/shard_map/convert_element_type | solution.py:22
  10.4 0.2 reshape.76
  10.6 1.7 %fusion = bf16[2,256,128]{1,2,0:T(8,128)(2,1)S(1)} fusion(f32[2,135,256]{2,1,0:T(8,128)S(1)} %reshape.76, f32[256]{0:T(256)S(1)} %bitcast.56, f32[256]{0:T(256)S(1)} %bitcast.58, f32[256]{0:T(256)S(1)} %bitcast.46, f32[256]{0:T(256)S(1)} %bitcast.48, f32[256]{0:T(256)S(1)} %bitcast.50, f32[256]{0:T(256)S(1)} %bitcast.52, f32[256]{0:T(256)S(1)} %bitcast.54, ...), kind=kOutput, calls=%fused_computation.4 | convolution fusion | flops 203489280 | bytes 2237952 | tf_op jit(solution)/shard_map/wn,asn->aws/dot_general | solution.py:28
  12.4 0.1 copy.15
  12.6 0.2 reshape.77
  12.8 1.7 %fusion.1 = bf16[2,256,128]{1,2,0:T(8,128)(2,1)S(1)} fusion(f32[2,135,256]{2,1,0:T(8,128)S(1)} %reshape.77, f32[256]{0:T(256)S(1)} %bitcast.57, f32[256]{0:T(256)S(1)} %bitcast.59, f32[256]{0:T(256)S(1)} %bitcast.47, f32[256]{0:T(256)S(1)} %bitcast.49, f32[256]{0:T(256)S(1)} %bitcast.51, f32[256]{0:T(256)S(1)} %bitcast.53, f32[256]{0:T(256)S(1)} %bitcast.55, ...), kind=kOutput, calls=%fused_computation.5 | convolution fusion | flops 203489280 | bytes 2237952 | tf_op jit(solution)/shard_map/wn,asn->aws/dot_general | solution.py:28
  14.5 0.1 copy.16
  14.7 0.7 pad_maximum_fusion.2
  15.5 0.0 all-gather.3.cloned.1.call-update
  15.5 32.9 %all-gather.3.cloned.1.call-done = bf16[8,128,512]{2,1,0:T(8,128)(2,1)} async-done(((bf16[2,128,512]{2,1,0:T(8,128)(2,1)}), bf16[8,128,512]{2,1,0:T(8,128)(2,1)}) %all-gather.3.cloned.1.call-update) | async-done | bytes 1048592 | tf_op jit(solution)/shard_map/all_gather | solution.py:58
  48.4 3.3 %copy.17 = bf16[4,2,128,512]{3,1,0,2:T(2,128)(2,1)} copy(bf16[4,2,128,512]{3,2,1,0:T(8,128)(2,1)} %bitcast.43) | data formatting | bytes 2097152 | tf_op jit(solution)/shard_map/all_gather | solution.py:58
  51.6 18.7 %all-to-all-start = ((bf16[4,2,128,512]{3,1,0,2:T(2,128)(2,1)}), bf16[4,2,128,512]{3,1,0,2:T(2,128)(2,1)S(1)}, u32[]{:S(2)}, u32[]{:S(2)}) async-start(bf16[4,2,128,512]{3,1,0,2:T(2,128)(2,1)} %copy.17), calls=%async_computation | async-start | bytes 2097152 | tf_op jit(solution)/shard_map/all_to_all | solution.py:59
  70.4 56.0 %all-to-all-done = bf16[4,2,128,512]{3,1,0,2:T(2,128)(2,1)S(1)} async-done(((bf16[4,2,128,512]{3,1,0,2:T(2,128)(2,1)}), bf16[4,2,128,512]{3,1,0,2:T(2,128)(2,1)S(1)}, u32[]{:S(2)}, u32[]{:S(2)}) %all-to-all-start) | async-done | bytes 1048608 | tf_op jit(solution)/shard_map/all_to_all | solution.py:59
  126.4 0.7 copy.19
  127.1 1.4 copy.18
  128.5 0.7 reshape_reshape.3
  129.2 0.4 reshape.74
  129.7 2.3 %slice_negate_fusion = (bf16[1024,1,2,1,128]{4,3,2,0,1:T(2,128)(2,1)S(1)}, bf16[1024,1,2,1,128]{4,3,2,0,1:T(2,128)(2,1)S(1)}) fusion(bf16[1024,1,2,2,128]{4,3,2,0,1:T(2,128)(2,1)S(1)} %reshape_reshape.3), kind=kLoop, calls=%fused_computation.6 | loop fusion | flops 262144 | bytes 2097152 | tf_op jit(solution)/shard_map/neg | solution.py:35
  132.0 2.4 %pad_maximum_fusion.1 = bf16[1024,1,2,2,128]{4,3,2,0,1:T(2,128)(2,1)S(1)} fusion(bf16[1024,1,2,1,128]{4,3,2,0,1:T(2,128)(2,1)S(1)} %get-tuple-element.8, bf16[1024,1,2,1,128]{4,3,2,0,1:T(2,128)(2,1)S(1)} %get-tuple-element.7), kind=kLoop, calls=%fused_computation.7 | loop fusion | flops 2097152 | bytes 2097152 | tf_op jit(solution)/shard_map/stack | solution.py:35
  134.5 0.4 reshape.75
  134.9 1.8 %constant_dynamic-slice_fusion = bf16[1,256,1,512]{3,0,1,2:T(2,128)(2,1)S(1)} fusion(bf16[4,256,1,512]{3,0,1,2:T(4,128)(2,1)} %bitcast.41, s32[]{:T(128)S(6)} %select_n.46), kind=kLoop, calls=%fused_computation.81 | loop fusion | bytes 524292 | tf_op jit(solution)/shard_map/jit(dynamic_index_in_dim)/dynamic_slice | solution.py:61
  136.7 0.1 pad_maximum_fusion
  136.8 2.1 %multiply_bitcast_fusion = f32[1,2,256,1024]{3,2,1,0:T(8,128)} fusion(bf16[2,1024,512]{2,1,0:T(8,128)(2,1)S(1)} %bitcast.40, bf16[1,256,1,512]{3,0,1,2:T(2,128)(2,1)S(1)} %constant_dynamic-slice_fusion), kind=kOutput, calls=%fused_computation.1 | convolution fusion | flops 537395200 | bytes 4456448 | tf_op jit(solution)/shard_map/cik,cjk->cij/dot_general | solution.py:41
  (4 shorter events, 0.1 us)
Async XLA Ops:
  6.5 41.8 %all-gather.3.cloned.1.call-start = ((), (), s32[]{:S(2)}) async-start(), calls=%async_computation.1 | async-start | bytes 1310720 | tf_op jit(solution)/shard_map/all_gather | solution.py:58
  51.6 74.8 %all-to-all-start = ((bf16[4,2,128,512]{3,1,0,2:T(2,128)(2,1)}), bf16[4,2,128,512]{3,1,0,2:T(2,128)(2,1)S(1)}, u32[]{:S(2)}, u32[]{:S(2)}) async-start(bf16[4,2,128,512]{3,1,0,2:T(2,128)(2,1)} %copy.17), calls=%async_computation | async-start | bytes 2097152 | tf_op jit(solution)/shard_map/all_to_all | solution.py:59
Sparse Core Ops, SparseCore 0:
  15.6 32.7 all-gather.2
where the time goes:
time: 146 us
  waiting for transfers between devices  88.9 us (61%)
  starting transfers between devices  18.7 us (13%)
  between operations  13.5 us (9%)
  local copies, waits for them, and re-layouts  10.5 us (7%)
  other arithmetic  8.5 us (6%)
  matrix products  5.56 us (4%)
    all_to_all x1, waiting for transfers between devices, shards(): lax.all_to_all(gathered, 'chan', split_axis=2, concat_axis=1, tiled=True)  56 us
    all_gather x1, waiting for transfers between devices, shards(): gathered = lax.all_gather(spectra, 'pair', axis=0, tiled=True)  32.9 us
    all_to_all x1, starting transfers between devices, shards(): lax.all_to_all(gathered, 'chan', split_axis=2, concat_axis=1, tiled=True)  18.7 us
    dot_general x2, matrix products, channelize(): jnp.einsum('wn,asn->aws', transform, filtered, precision=lax.Precision.HI...  3.49 us
    all_gather x1, local copies, waits for them, and re-layouts, shards(): gathered = lax.all_gather(spectra, 'pair', axis=0, tiled=True)  3.27 us
  transfers between devices with their start and end apart: 2, of which 2 were waited for; matrix products, arithmetic and copies ran while one was open for 0% of the time, Pallas kernels for 0%

commit v1 on v0

--- a/solution.py
+++ b/solution.py
@@ -3,6 +3,19 @@
 import jax.numpy as jnp
 from jax import lax
 from jax.sharding import PartitionSpec as P
+
+
+def cubes_choose(point, mesh_name, dim_k):
+    state_now = jnp.concatenate(
+        jax.lax.all_to_all(
+            jnp.stack([point] * jax.lax.axis_size(mesh_name)),
+            split_axis=0,
+            axis_name=mesh_name,
+            concat_axis=0,
+        ),
+        axis=dim_k,
+    )
+    return state_now
 
 
 def dft_rows(channels):
@@ -55,7 +68,7 @@
         for batch in range(batch_count)
     ]
     spectra = jnp.concatenate(pieces, axis=2)[None]
-    gathered = lax.all_gather(spectra, "pair", axis=0, tiled=True)
+    gathered = cubes_choose(spectra, "pair", 0)
     turned = lax.all_to_all(gathered, "chan", split_axis=2, concat_axis=1, tiled=True)
     everyone = turned.reshape(turned.shape[0] * turned.shape[1], turned.shape[2], turned.shape[3])
     own_rows = lax.dynamic_index_in_dim(turned, lax.axis_index("pair"), 0, keepdims=False)

time: 146 us -> 118 us (0.81)
  waiting for transfers between devices: 88.9 us -> 55.2 us
  blocking collectives: 0 us -> 17 us
  between operations: 13.5 us -> 0.15 us
  starting transfers between devices: 18.7 us -> 21.9 us
    all_gather x1 -> x0, waiting for transfers between devices: 32.9 us -> none  [shards(): gathered = lax.all_gather(spectra, 'pair', axis=0, tiled=True)]
    all_to_all x0 -> x1, blocking collectives: none -> 17 us  [cubes_choose(): jax.lax.all_to_all(jnp.stack([point] * jax.lax.axis_size(mesh_name)), spl...]
    all_gather x1 -> x0, local copies, waits for them, and re-layouts: 3.27 us -> none  [shards(): gathered = lax.all_gather(spectra, 'pair', axis=0, tiled=True)]
    all_to_all x1, starting transfers between devices: 18.7 us -> 21.9 us  [shards(): lax.all_to_all(gathered, 'chan', split_axis=2, concat_axis=1, tiled=True)]
    reshape x0 -> x1, local copies, waits for them, and re-layouts: none -> 1.69 us  [cubes_choose(): jnp.concatenate(jax.lax.all_to_all(jnp.stack([point] * jax.lax.axis_size(...]
  transfers between devices with their start and end apart: 2 -> 1, of which waited for: 2 -> 1; matrix products, arithmetic and copies ran while one was open for 0% -> 0% of each run, Pallas kernels for 0% -> 0%
where the time goes in v1:
time: 118 us; the launch traced here: 117 us
  waiting for transfers between devices  55.2 us (47%)
  starting transfers between devices  21.9 us (19%)
  blocking collectives  17 us (14%)
  local copies, waits for them, and re-layouts  9.74 us (8%)
  other arithmetic  7.79 us (7%)
  matrix products  5.56 us (5%)
    all_to_all x1, waiting for transfers between devices, shards(): lax.all_to_all(gathered, 'chan', split_axis=2, concat_axis=1, tiled=True)  55.2 us
    all_to_all x1, starting transfers between devices, shards(): lax.all_to_all(gathered, 'chan', split_axis=2, concat_axis=1, tiled=True)  21.9 us
    all_to_all x1, blocking collectives, cubes_choose(): jax.lax.all_to_all(jnp.stack([point] * jax.lax.axis_size(mesh_name)), spl...  17 us
    dot_general x2, matrix products, channelize(): jnp.einsum('wn,asn->aws', transform, filtered, precision=lax.Precision.HI...  3.49 us
    convert_element_type x1, other arithmetic, channelize(): sample_rows.astype(jnp.float32)  2.85 us
    another operation x1, other arithmetic, correlate(): jnp.stack([-shaped[:, :, :, 1, :], shaped[:, :, :, 0, :]], axis=3)  2.43 us
  transfers between devices with their start and end apart: 1, of which 1 were waited for; matrix products, arithmetic and copies ran while one was open for 0% of the time, Pallas kernels for 0%

profile of v1, /device:TPU:8, one launch (start us, length us, event | category | flops | bytes accessed | tf_op | source)
XLA Modules:
  0.0 117.5 jit_solution(9442558519951687002)
XLA Ops:
  0.0 1.0 fusion.70
  1.0 2.8 %fusion.3 = (f32[2,34560]{1,0:T(2,128)S(1)}, f32[2,34560]{1,0:T(2,128)S(1)}) fusion(bf16[2,2,34560]{2,1,0:T(2,128)(2,1)} %bitcast.43), kind=kLoop, calls=%fused_computation.14 | loop fusion | flops 138240 | bytes 829440 | tf_op jit(solution)/shard_map/convert_element_type | solution.py:35
  3.9 0.2 reshape.82
  4.1 1.7 %fusion = bf16[2,256,128]{1,2,0:T(8,128)(2,1)S(1)} fusion(f32[2,135,256]{2,1,0:T(8,128)S(1)} %reshape.82, f32[256]{0:T(256)S(1)} %bitcast.56, f32[256]{0:T(256)S(1)} %bitcast.58, f32[256]{0:T(256)S(1)} %bitcast.46, f32[256]{0:T(256)S(1)} %bitcast.48, f32[256]{0:T(256)S(1)} %bitcast.50, f32[256]{0:T(256)S(1)} %bitcast.52, f32[256]{0:T(256)S(1)} %bitcast.54, ...), kind=kOutput, calls=%fused_computation.4 | convolution fusion | flops 203489280 | bytes 2237952 | tf_op jit(solution)/shard_map/wn,asn->aws/dot_general | solution.py:41
  5.8 0.1 copy.17
  6.0 0.2 reshape.83
  6.3 1.7 %fusion.1 = bf16[2,256,128]{1,2,0:T(8,128)(2,1)S(1)} fusion(f32[2,135,256]{2,1,0:T(8,128)S(1)} %reshape.83, f32[256]{0:T(256)S(1)} %bitcast.57, f32[256]{0:T(256)S(1)} %bitcast.59, f32[256]{0:T(256)S(1)} %bitcast.47, f32[256]{0:T(256)S(1)} %bitcast.49, f32[256]{0:T(256)S(1)} %bitcast.51, f32[256]{0:T(256)S(1)} %bitcast.53, f32[256]{0:T(256)S(1)} %bitcast.55, ...), kind=kOutput, calls=%fused_computation.5 | convolution fusion | flops 203489280 | bytes 2237952 | tf_op jit(solution)/shard_map/wn,asn->aws/dot_general | solution.py:41
  8.0 0.1 copy.18
  8.2 0.3 copy.19
  8.5 0.5 stack.7
  9.0 17.0 %all_to_all.23 = bf16[4,1,2,128,512]{4,2,3,1,0:T(2,128)(2,1)S(1)} all-to-all(bf16[4,1,2,128,512]{4,2,3,1,0:T(2,128)(2,1)S(1)} %stack.7), channel_id=1, replica_groups=mesh['chan'=128,'pair'=4] {'pair'}, dimensions={0} | all-to-all | bytes 2097152 | tf_op jit(solution)/shard_map/all_to_all | solution.py:10
  26.1 1.7 %copy.20 = bf16[4,2,128,512]{3,1,0,2:T(2,128)(2,1)} copy(bf16[4,2,128,512]{3,1,2,0:T(2,128)(2,1)S(1)} %bitcast.41) | data formatting | bytes 2097152 | tf_op jit(solution)/shard_map/reshape | solution.py:9
  27.8 21.9 %all-to-all-start.1 = ((bf16[4,2,128,512]{3,1,0,2:T(2,128)(2,1)}), bf16[4,2,128,512]{3,1,0,2:T(2,128)(2,1)S(1)}, u32[]{:S(2)}, u32[]{:S(2)}) async-start(bf16[4,2,128,512]{3,1,0,2:T(2,128)(2,1)} %copy.20), calls=%async_computation.1 | async-start | bytes 2097152 | tf_op jit(solution)/shard_map/all_to_all | solution.py:72
  49.7 55.2 %all-to-all-done.1 = bf16[4,2,128,512]{3,1,0,2:T(2,128)(2,1)S(1)} async-done(((bf16[4,2,128,512]{3,1,0,2:T(2,128)(2,1)}), bf16[4,2,128,512]{3,1,0,2:T(2,128)(2,1)S(1)}, u32[]{:S(2)}, u32[]{:S(2)}) %all-to-all-start.1) | async-done | bytes 1048608 | tf_op jit(solution)/shard_map/all_to_all | solution.py:72
  105.0 0.7 copy.22
  105.7 1.4 %copy.21 = bf16[4,128,2,1,512]{4,0,2,1,3:T(4,128)(2,1)} copy(bf16[4,128,2,1,512]{4,2,0,1,3:T(2,128)(2,1)S(1)} %bitcast.39) | data formatting | bytes 2097152 | tf_op jit(solution)/shard_map/all_to_all | solution.py:72
  107.1 0.7 reshape_reshape.3
  107.8 0.4 reshape.80
  108.2 2.3 %slice_negate_fusion = (bf16[1024,1,2,1,128]{4,3,2,0,1:T(2,128)(2,1)S(1)}, bf16[1024,1,2,1,128]{4,3,2,0,1:T(2,128)(2,1)S(1)}) fusion(bf16[1024,1,2,2,128]{4,3,2,0,1:T(2,128)(2,1)S(1)} %reshape_reshape.3), kind=kLoop, calls=%fused_computation.6 | loop fusion | flops 262144 | bytes 2097152 | tf_op jit(solution)/shard_map/neg | solution.py:48
  110.6 2.4 %pad_maximum_fusion.1 = bf16[1024,1,2,2,128]{4,3,2,0,1:T(2,128)(2,1)S(1)} fusion(bf16[1024,1,2,1,128]{4,3,2,0,1:T(2,128)(2,1)S(1)} %get-tuple-element.8, bf16[1024,1,2,1,128]{4,3,2,0,1:T(2,128)(2,1)S(1)} %get-tuple-element.7), kind=kLoop, calls=%fused_computation.7 | loop fusion | flops 2097152 | bytes 2097152 | tf_op jit(solution)/shard_map/stack | solution.py:48
  113.0 0.4 reshape.81
  113.5 1.8 %constant_dynamic-slice_fusion = bf16[1,256,1,512]{3,0,1,2:T(2,128)(2,1)S(1)} fusion(bf16[4,256,1,512]{3,0,1,2:T(4,128)(2,1)} %bitcast.42, s32[]{:T(128)S(6)} %select_n.46), kind=kLoop, calls=%fused_computation.81 | loop fusion | bytes 524292 | tf_op jit(solution)/shard_map/jit(dynamic_index_in_dim)/dynamic_slice | solution.py:74
  115.2 0.1 pad_maximum_fusion
  115.4 2.1 %multiply_bitcast_fusion = f32[1,2,256,1024]{3,2,1,0:T(8,128)} fusion(bf16[2,1024,512]{2,1,0:T(8,128)(2,1)S(1)} %bitcast.40, bf16[1,256,1,512]{3,0,1,2:T(2,128)(2,1)S(1)} %constant_dynamic-slice_fusion), kind=kOutput, calls=%fused_computation.1 | convolution fusion | flops 537395200 | bytes 4456448 | tf_op jit(solution)/shard_map/cik,cjk->cij/dot_general | solution.py:54
  (5 shorter events, 0.1 us)
Async XLA Ops:
  27.8 77.2 %all-to-all-start.1 = ((bf16[4,2,128,512]{3,1,0,2:T(2,128)(2,1)}), bf16[4,2,128,512]{3,1,0,2:T(2,128)(2,1)S(1)}, u32[]{:S(2)}, u32[]{:S(2)}) async-start(bf16[4,2,128,512]{3,1,0,2:T(2,128)(2,1)} %copy.20), calls=%async_computation.1 | async-start | bytes 2097152 | tf_op jit(solution)/shard_map/all_to_all | solution.py:72
